TPU v7x, 256 devices: a whole 4x4x8 slice. The times are simulated.
256 devices in a mesh: gen: 32 (over y, x, core), beam: 8 (over z).
Axes of the slice: x: 4, y: 4, z: 8, core: 2. Of those that a mesh axis runs over, the one named last changes fastest.
Arguments:
- gen_showers: bfloat16 [32768, 256], P('gen'), may hold values from -12 to 12
- beam_showers: bfloat16 [16384, 256], P('beam'), may hold values from -6 to 6
- embed_weight: bfloat16 [256, 128], replicated, may hold values from -0.375 to 0.375
- eps_roster: float32 [4], replicated, may hold values from 0.04 to 0.08
Outputs:
- gen_potential: float32 [32768], P('gen')
- beam_potential: float32 [16384], P('beam')
- weight_grad: float32 [256, 128], replicated
All inputs are finite; a program needn't handle non-finite values.
Results may differ from a plain program's by a relative error of at most 0.03.
Values sent between devices are 32-bit elements; how exact they have to be, the bound alone decides.
No kernel may reach another device: no remote copies, remote signals or barrier semaphores. Data moves between devices by JAX's collectives and lax.ppermute only.
A program may use at most 64 MiB of HBM per device.

v0:
```python
import math
import jax
import jax.numpy as jnp
from jax import lax
from jax.sharding import PartitionSpec as P

SWEEPS = 4


def embed(showers, weight):
    act = jnp.tanh(jnp.dot(showers, weight, preferred_element_type=jnp.float32))
    return (act, act.astype(jnp.bfloat16))


def tile_cost(gen_emb, beam_emb, gen_sq, beam_sq):
    cross = lax.dot_general(
        gen_emb, beam_emb, (((1,), (1,)), ((), ())), preferred_element_type=jnp.float32
    )
    return gen_sq[:, None] + beam_sq[None, :] - 2.0 * cross


def row_lse(scores):
    top = lax.pmax(jnp.max(scores, axis=1), "beam")
    total = lax.psum(jnp.sum(jnp.exp(scores - top[:, None]), axis=1), "beam")
    return top + jnp.log(total)


def col_lse(scores):
    top = lax.pmax(jnp.max(scores, axis=0), "gen")
    total = lax.psum(jnp.sum(jnp.exp(scores - top[None, :]), axis=0), "gen")
    return top + jnp.log(total)


def transpose_dot(left, right):
    return lax.dot_general(
        left.astype(jnp.float32),
        right,
        (((0,), (0,)), ((), ())),
        precision=lax.Precision.HIGHEST,
        preferred_element_type=jnp.float32,
    )


def on_device(gen_showers, beam_showers, embed_weight, eps_roster):
    gen_act, gen_emb = embed(gen_showers, embed_weight)
    beam_act, beam_emb = embed(beam_showers, embed_weight)
    gen_float = gen_emb.astype(jnp.float32)
    beam_float = beam_emb.astype(jnp.float32)
    gen_sq = jnp.sum(gen_float * gen_float, axis=1)
    beam_sq = jnp.sum(beam_float * beam_float, axis=1)
    rows = gen_emb.shape[0]
    columns = beam_emb.shape[0]
    log_beam = math.log(columns * lax.axis_size("beam"))
    log_gen = math.log(rows * lax.axis_size("gen"))
    beam_pot = jnp.zeros((columns,), jnp.float32)
    gen_pot = jnp.zeros((rows,), jnp.float32)
    for sweep in range(SWEEPS):
        temper = eps_roster[sweep]
        cost = tile_cost(gen_emb, beam_emb, gen_sq, beam_sq)
        gen_pot = temper * (log_beam - row_lse((beam_pot[None, :] - cost) / temper))
        cost = tile_cost(gen_emb, beam_emb, gen_sq, beam_sq)
        beam_pot = temper * (log_gen - col_lse((gen_pot[:, None] - cost) / temper))
    last = eps_roster[SWEEPS - 1]
    cost = tile_cost(gen_emb, beam_emb, gen_sq, beam_sq)
    mass = jnp.exp((gen_pot[:, None] + beam_pot[None, :] - cost) / last - log_beam)
    plan = mass.astype(jnp.bfloat16)
    gen_count = rows // lax.axis_size("beam")
    part = plan
    row_mass = jnp.sum(mass, axis=1)
    own = gen_float
    moved = jnp.dot(part, beam_emb, preferred_element_type=jnp.float32)
    grad_gen = lax.psum_scatter(
        2.0 * (row_mass[:, None] * own - moved), "beam", scatter_dimension=0, tiled=True
    )
    gen_start = lax.axis_index("beam") * gen_count
    act_rows = lax.dynamic_slice_in_dim(gen_act, gen_start, gen_count, 0)
    shower_rows = lax.dynamic_slice_in_dim(gen_showers, gen_start, gen_count, 0)
    beam_count = columns // lax.axis_size("gen")
    part = plan
    col_mass = jnp.sum(mass, axis=0)
    own = beam_float
    moved = lax.dot_general(
        part, gen_emb, (((0,), (0,)), ((), ())), preferred_element_type=jnp.float32
    )
    grad_beam = lax.psum_scatter(
        2.0 * (col_mass[:, None] * own - moved), "gen", scatter_dimension=0, tiled=True
    )
    beam_start = lax.axis_index("gen") * beam_count
    act_cols = lax.dynamic_slice_in_dim(beam_act, beam_start, beam_count, 0)
    shower_cols = lax.dynamic_slice_in_dim(beam_showers, beam_start, beam_count, 0)
    partial_grad = transpose_dot(shower_rows, grad_gen * (1.0 - act_rows * act_rows))
    partial_grad = partial_grad + transpose_dot(
        shower_cols, grad_beam * (1.0 - act_cols * act_cols)
    )
    weight_grad = lax.psum(partial_grad, ("gen", "beam"))
    return (gen_pot, beam_pot, weight_grad)


def solution(mesh):
    in_specs = (P("gen", None), P("beam", None), P(), P())
    out_specs = (P("gen"), P("beam"), P())
    return jax.shard_map(
        on_device, mesh=mesh, in_specs=in_specs, out_specs=out_specs, check_vma=False
    )
```

profile of v0, /device:TPU:8, one launch (start us, length us, event | category | flops | bytes accessed | tf_op | source)
XLA Modules:
  0.0 1114.6 jit_solution(14821040143072383777)
XLA Ops:
  7.2 0.0 copy-start
  7.2 0.0 reduce-scatter.5.cloned.1.call-start
  7.2 1.4 fusion.38
  8.6 1.4 fusion.14
  10.0 1.4 fusion.19
  11.4 5.3 fusion
  16.7 20.0 %pmax.56 = f32[1024]{0:T(1024)S(1)} all-reduce(f32[1024]{0:T(1024)S(1)} %get-tuple-element.16), channel_id=1, replica_groups=mesh['gen'=32,'beam'=8] {'beam'}, use_global_device_ids=true, to_apply=%region_3.0 | all-reduce | flops 1024 | bytes 8192 | tf_op jit(solution)/shard_map/pmax | solution.py:23
  36.7 5.1 exponential_reduce_fusion.7
  41.8 14.2 %psum.63 = f32[1024]{0:T(1024)S(1)} all-reduce(f32[1024]{0:T(1024)S(1)} %exponential_reduce_fusion.7), channel_id=1, replica_groups=mesh['gen'=32,'beam'=8] {'beam'}, use_global_device_ids=true, to_apply=%region_5.0 | all-reduce | flops 1024 | bytes 8192 | tf_op jit(solution)/shard_map/psum | solution.py:24
  56.0 0.7 subtract_multiply_fusion.7
  56.6 4.7 fusion.15
  61.3 54.0 %pmax.57 = f32[2048]{0:T(1024)S(1)} all-reduce(f32[2048]{0:T(1024)S(1)} %fusion.15), channel_id=1, replica_groups=mesh['gen'=32,'beam'=8] {'gen'}, use_global_device_ids=true, to_apply=%region_7.0 | all-reduce | flops 2048 | bytes 16384 | tf_op jit(solution)/shard_map/pmax | solution.py:29
  115.4 5.2 exponential_reduce_fusion.6
  120.5 55.5 %psum.64 = f32[2048]{0:T(1024)S(1)} all-reduce(f32[2048]{0:T(1024)S(1)} %exponential_reduce_fusion.6), channel_id=1, replica_groups=mesh['gen'=32,'beam'=8] {'gen'}, use_global_device_ids=true, to_apply=%region_9.0 | all-reduce | flops 2048 | bytes 16384 | tf_op jit(solution)/shard_map/psum | solution.py:30
  176.0 0.7 subtract_multiply_fusion.3
  176.7 4.8 fusion.1
  181.5 16.2 %pmax.58 = f32[1024]{0:T(1024)S(1)} all-reduce(f32[1024]{0:T(1024)S(1)} %fusion.1), channel_id=1, replica_groups=mesh['gen'=32,'beam'=8] {'beam'}, use_global_device_ids=true, to_apply=%region_11.0 | all-reduce | flops 1024 | bytes 8192 | tf_op jit(solution)/shard_map/pmax | solution.py:23
  197.7 5.1 exponential_reduce_fusion.5
  202.8 14.2 %psum.65 = f32[1024]{0:T(1024)S(1)} all-reduce(f32[1024]{0:T(1024)S(1)} %exponential_reduce_fusion.5), channel_id=1, replica_groups=mesh['gen'=32,'beam'=8] {'beam'}, use_global_device_ids=true, to_apply=%region_13.0 | all-reduce | flops 1024 | bytes 8192 | tf_op jit(solution)/shard_map/psum | solution.py:24
  217.0 0.6 subtract_multiply_fusion.6
  217.5 4.6 fusion.16
  222.1 63.7 %pmax.59 = f32[2048]{0:T(1024)S(1)} all-reduce(f32[2048]{0:T(1024)S(1)} %fusion.16), channel_id=1, replica_groups=mesh['gen'=32,'beam'=8] {'gen'}, use_global_device_ids=true, to_apply=%region_15.0 | all-reduce | flops 2048 | bytes 16384 | tf_op jit(solution)/shard_map/pmax | solution.py:29
  285.8 5.1 exponential_reduce_fusion.4
  290.9 63.7 %psum.66 = f32[2048]{0:T(1024)S(1)} all-reduce(f32[2048]{0:T(1024)S(1)} %exponential_reduce_fusion.4), channel_id=1, replica_groups=mesh['gen'=32,'beam'=8] {'gen'}, use_global_device_ids=true, to_apply=%region_17.0 | all-reduce | flops 2048 | bytes 16384 | tf_op jit(solution)/shard_map/psum | solution.py:30
  354.6 0.6 subtract_multiply_fusion.2
  355.2 4.9 fusion.2
  360.1 16.2 %pmax.60 = f32[1024]{0:T(1024)S(1)} all-reduce(f32[1024]{0:T(1024)S(1)} %fusion.2), channel_id=1, replica_groups=mesh['gen'=32,'beam'=8] {'beam'}, use_global_device_ids=true, to_apply=%region_19.0 | all-reduce | flops 1024 | bytes 8192 | tf_op jit(solution)/shard_map/pmax | solution.py:23
  376.3 5.1 exponential_reduce_fusion.3
  381.4 14.3 %psum.67 = f32[1024]{0:T(1024)S(1)} all-reduce(f32[1024]{0:T(1024)S(1)} %exponential_reduce_fusion.3), channel_id=1, replica_groups=mesh['gen'=32,'beam'=8] {'beam'}, use_global_device_ids=true, to_apply=%region_21.0 | all-reduce | flops 1024 | bytes 8192 | tf_op jit(solution)/shard_map/psum | solution.py:24
  395.8 0.7 subtract_multiply_fusion.5
  396.4 4.7 fusion.17
  401.1 63.7 %pmax.61 = f32[2048]{0:T(1024)S(1)} all-reduce(f32[2048]{0:T(1024)S(1)} %fusion.17), channel_id=1, replica_groups=mesh['gen'=32,'beam'=8] {'gen'}, use_global_device_ids=true, to_apply=%region_23.0 | all-reduce | flops 2048 | bytes 16384 | tf_op jit(solution)/shard_map/pmax | solution.py:29
  464.8 5.2 exponential_reduce_fusion.2
  470.0 63.7 %psum.68 = f32[2048]{0:T(1024)S(1)} all-reduce(f32[2048]{0:T(1024)S(1)} %exponential_reduce_fusion.2), channel_id=1, replica_groups=mesh['gen'=32,'beam'=8] {'gen'}, use_global_device_ids=true, to_apply=%region_25.0 | all-reduce | flops 2048 | bytes 16384 | tf_op jit(solution)/shard_map/psum | solution.py:30
  533.6 0.7 subtract_multiply_fusion.1
  534.3 4.9 fusion.3
  539.2 16.2 %pmax.62 = f32[1024]{0:T(1024)S(1)} all-reduce(f32[1024]{0:T(1024)S(1)} %fusion.3), channel_id=1, replica_groups=mesh['gen'=32,'beam'=8] {'beam'}, use_global_device_ids=true, to_apply=%region_27.0 | all-reduce | flops 1024 | bytes 8192 | tf_op jit(solution)/shard_map/pmax | solution.py:23
  555.4 5.1 exponential_reduce_fusion.1
  560.5 14.2 %psum.69 = f32[1024]{0:T(1024)S(1)} all-reduce(f32[1024]{0:T(1024)S(1)} %exponential_reduce_fusion.1), channel_id=1, replica_groups=mesh['gen'=32,'beam'=8] {'beam'}, use_global_device_ids=true, to_apply=%region_29.0 | all-reduce | flops 1024 | bytes 8192 | tf_op jit(solution)/shard_map/psum | solution.py:24
  574.7 0.7 subtract_multiply_fusion.4
  575.4 0.0 copy-start.2
  575.4 4.7 fusion.18
  580.0 63.7 %pmax.63 = f32[2048]{0:T(1024)S(1)} all-reduce(f32[2048]{0:T(1024)S(1)} %fusion.18), channel_id=1, replica_groups=mesh['gen'=32,'beam'=8] {'gen'}, use_global_device_ids=true, to_apply=%region_31.0 | all-reduce | flops 2048 | bytes 16384 | tf_op jit(solution)/shard_map/pmax | solution.py:29
  643.7 5.2 exponential_reduce_fusion
  648.9 63.7 %psum.70 = f32[2048]{0:T(1024)S(1)} all-reduce(f32[2048]{0:T(1024)S(1)} %exponential_reduce_fusion), channel_id=1, replica_groups=mesh['gen'=32,'beam'=8] {'gen'}, use_global_device_ids=true, to_apply=%region_33.0 | all-reduce | flops 2048 | bytes 16384 | tf_op jit(solution)/shard_map/psum | solution.py:30
  712.6 0.7 subtract_multiply_fusion
  713.3 0.0 copy-done.2
  713.3 0.0 copy-start.3
  713.3 5.7 fusion.37
  719.0 0.0 copy-start.1
  719.0 1.9 copy-done.1
  720.9 2.4 fusion.4
  723.3 0.0 reduce-scatter.5.cloned.1.call-update
  723.3 0.0 reduce-scatter.3.cloned.1.call-start
  723.4 4.5 fusion.11
  727.9 0.0 reduce-scatter.3.cloned.1.call-update
  727.9 0.0 all-reduce.2.cloned.1.call-start
  728.0 92.3 %reduce-scatter.5.cloned.1.call-done = f32[64,128]{1,0:T(8,128)} async-done(((f32[2048,128]{1,0:T(8,128)}), f32[64,128]{1,0:T(8,128)}) %reduce-scatter.5.cloned.1.call-update) | async-done | bytes 32784 | tf_op jit(solution)/shard_map/reduce_scatter | solution.py:85
  820.2 1.0 fusion.25
  821.3 38.7 %reduce-scatter.3.cloned.1.call-done = f32[128,128]{0,1:T(8,128)} async-done(((f32[1024,128]{0,1:T(8,128)}), f32[128,128]{0,1:T(8,128)}) %reduce-scatter.3.cloned.1.call-update) | async-done | bytes 65552 | tf_op jit(solution)/shard_map/reduce_scatter | solution.py:72
  859.9 1.8 convolution_add_fusion
  861.7 0.0 all-reduce.2.cloned.1.call-update
  861.7 244.8 %all-reduce.2.cloned.1.call-done = f32[256,128]{1,0:T(8,128)} async-done(((f32[256,128]{1,0:T(8,128)}), f32[256,128]{1,0:T(8,128)}) %all-reduce.2.cloned.1.call-update) | async-done | bytes 131088 | tf_op jit(solution)/shard_map/psum | solution.py:95
  1106.5 1.6 copy.8
  (2 shorter events, 0.0 us)
Async XLA Ops:
  7.2 1.5 copy-start
  7.2 813.0 %reduce-scatter.5.cloned.1.call-start = ((), (), s32[]{:S(2)}) async-start(), calls=%async_computation.3 | async-start | bytes 1081344 | tf_op jit(solution)/shard_map/reduce_scatter | solution.py:85
  575.4 137.9 %copy-start.2 = (f32[1024]{0:T(1024)}, f32[1024]{0:T(1024)S(1)}, u32[]{:S(2)}) copy-start(f32[1024]{0:T(1024)S(1)} %subtract_multiply_fusion.4) | copy-start | bytes 12292
  713.3 10.0 copy-start.3
  719.0 1.9 copy-start.1
  723.3 136.6 %reduce-scatter.3.cloned.1.call-start = ((), (), s32[]{:S(2)}) async-start(), calls=%async_computation.2 | async-start | bytes 589824 | tf_op jit(solution)/shard_map/reduce_scatter | solution.py:72
  727.9 378.6 %all-reduce.2.cloned.1.call-start = ((), (), s32[]{:S(2)}) async-start(), calls=%async_computation.4 | async-start | bytes 262144 | tf_op jit(solution)/shard_map/psum | solution.py:95
Sparse Core Ops, SparseCore 0:
  723.5 96.7 reduce-scatter.4
  822.9 36.9 reduce-scatter.2
  866.0 240.4 all-reduce.1
where the time goes:
time: 1120 us; the launch traced here: 1110 us
  blocking collectives  617 us (55%)
  waiting for transfers between devices  376 us (34%)
  other arithmetic  85 us (8%)
  matrix products  17.8 us (2%)
  between operations  14 us (1%)
    psum x4, blocking collectives, col_lse(): total = lax.psum(jnp.sum(jnp.exp(scores - top[None, :]), axis=0), 'gen')  247 us
    pmax x4, blocking collectives, col_lse(): top = lax.pmax(jnp.max(scores, axis=0), 'gen')  245 us
    psum x1, waiting for transfers between devices, on_device(): weight_grad = lax.psum(partial_grad, ('gen', 'beam'))  245 us
    reduce_scatter x1, waiting for transfers between devices, on_device(): lax.psum_scatter(2.0 * (col_mass[:, None] * own - moved), 'gen', scatter_...  92.3 us
    pmax x4, blocking collectives, row_lse(): top = lax.pmax(jnp.max(scores, axis=1), 'beam')  68.5 us
    psum x4, blocking collectives, row_lse(): total = lax.psum(jnp.sum(jnp.exp(scores - top[:, None]), axis=1), 'beam')  56.8 us
    reduce_scatter x1, waiting for transfers between devices, on_device(): lax.psum_scatter(2.0 * (row_mass[:, None] * own - moved), 'beam', scatter...  38.7 us
  transfers between devices with their start and end apart: 3, of which 3 were waited for; matrix products, arithmetic and copies ran while one was open for 0% of the time, Pallas kernels for 0%

commit v1 on v0

--- a/solution.py
+++ b/solution.py
@@ -92,7 +92,7 @@
     partial_grad = partial_grad + transpose_dot(
         shower_cols, grad_beam * (1.0 - act_cols * act_cols)
     )
-    weight_grad = lax.psum(partial_grad, ("gen", "beam"))
+    weight_grad = lax.psum(lax.psum(partial_grad, "beam"), "gen")
     return (gen_pot, beam_pot, weight_grad)
 
 

time: 1120 us -> 1060 us (0.946)
  waiting for transfers between devices: 376 us -> 314 us
    psum x1 -> x2, waiting for transfers between devices: 245 us -> 183 us  [on_device(): weight_grad = lax.psum(lax.psum(partial_grad, 'beam'), 'gen')]
  transfers between devices with their start and end apart: 3 -> 4, of which waited for: 3 -> 4; matrix products, arithmetic and copies ran while one was open for 0% -> 1% of each run, Pallas kernels for 0% -> 0%
where the time goes in v1:
time: 1060 us; the launch traced here: 1050 us
  blocking collectives  617 us (58%)
  waiting for transfers between devices  314 us (30%)
  other arithmetic  85 us (8%)
  matrix products  17.8 us (2%)
  between operations  14 us (1%)
    psum x4, blocking collectives, col_lse(): total = lax.psum(jnp.sum(jnp.exp(scores - top[None, :]), axis=0), 'gen')  247 us
    pmax x4, blocking collectives, col_lse(): top = lax.pmax(jnp.max(scores, axis=0), 'gen')  245 us
    psum x2, waiting for transfers between devices, on_device(): weight_grad = lax.psum(lax.psum(partial_grad, 'beam'), 'gen')  183 us
    reduce_scatter x1, waiting for transfers between devices, on_device(): lax.psum_scatter(2.0 * (col_mass[:, None] * own - moved), 'gen', scatter_...  92.3 us
    pmax x4, blocking collectives, row_lse(): top = lax.pmax(jnp.max(scores, axis=1), 'beam')  68.5 us
    psum x4, blocking collectives, row_lse(): total = lax.psum(jnp.sum(jnp.exp(scores - top[:, None]), axis=1), 'beam')  56.8 us
    reduce_scatter x1, waiting for transfers between devices, on_device(): lax.psum_scatter(2.0 * (row_mass[:, None] * own - moved), 'beam', scatter...  38.7 us
  transfers between devices with their start and end apart: 4, of which 4 were waited for; matrix products, arithmetic and copies ran while one was open for 1% of the time, Pallas kernels for 0%

profile of v1, /device:TPU:8, one launch (start us, length us, event | category | flops | bytes accessed | tf_op | source)
XLA Modules:
  0.0 1052.6 jit_solution(6541852075510185726)
XLA Ops:
  7.2 0.0 copy-start
  7.2 0.0 reduce-scatter.5.cloned.1.call-start
  7.2 1.4 fusion.38
  8.6 1.4 fusion.14
  10.0 1.4 fusion.19
  11.4 5.3 fusion
  16.7 20.0 %pmax.56 = f32[1024]{0:T(1024)S(1)} all-reduce(f32[1024]{0:T(1024)S(1)} %get-tuple-element.16), channel_id=1, replica_groups=mesh['gen'=32,'beam'=8] {'beam'}, use_global_device_ids=true, to_apply=%region_3.0 | all-reduce | flops 1024 | bytes 8192 | tf_op jit(solution)/shard_map/pmax | solution.py:23
  36.7 5.1 exponential_reduce_fusion.7
  41.8 14.2 %psum.70 = f32[1024]{0:T(1024)S(1)} all-reduce(f32[1024]{0:T(1024)S(1)} %exponential_reduce_fusion.7), channel_id=1, replica_groups=mesh['gen'=32,'beam'=8] {'beam'}, use_global_device_ids=true, to_apply=%region_5.0 | all-reduce | flops 1024 | bytes 8192 | tf_op jit(solution)/shard_map/psum | solution.py:24
  56.0 0.7 subtract_multiply_fusion.7
  56.6 4.7 fusion.15
  61.3 54.0 %pmax.57 = f32[2048]{0:T(1024)S(1)} all-reduce(f32[2048]{0:T(1024)S(1)} %fusion.15), channel_id=1, replica_groups=mesh['gen'=32,'beam'=8] {'gen'}, use_global_device_ids=true, to_apply=%region_7.0 | all-reduce | flops 2048 | bytes 16384 | tf_op jit(solution)/shard_map/pmax | solution.py:29
  115.4 5.2 exponential_reduce_fusion.6
  120.5 55.5 %psum.71 = f32[2048]{0:T(1024)S(1)} all-reduce(f32[2048]{0:T(1024)S(1)} %exponential_reduce_fusion.6), channel_id=1, replica_groups=mesh['gen'=32,'beam'=8] {'gen'}, use_global_device_ids=true, to_apply=%region_9.0 | all-reduce | flops 2048 | bytes 16384 | tf_op jit(solution)/shard_map/psum | solution.py:30
  176.0 0.7 subtract_multiply_fusion.3
  176.7 4.8 fusion.1
  181.5 16.2 %pmax.58 = f32[1024]{0:T(1024)S(1)} all-reduce(f32[1024]{0:T(1024)S(1)} %fusion.1), channel_id=1, replica_groups=mesh['gen'=32,'beam'=8] {'beam'}, use_global_device_ids=true, to_apply=%region_11.0 | all-reduce | flops 1024 | bytes 8192 | tf_op jit(solution)/shard_map/pmax | solution.py:23
  197.7 5.1 exponential_reduce_fusion.5
  202.8 14.2 %psum.72 = f32[1024]{0:T(1024)S(1)} all-reduce(f32[1024]{0:T(1024)S(1)} %exponential_reduce_fusion.5), channel_id=1, replica_groups=mesh['gen'=32,'beam'=8] {'beam'}, use_global_device_ids=true, to_apply=%region_13.0 | all-reduce | flops 1024 | bytes 8192 | tf_op jit(solution)/shard_map/psum | solution.py:24
  217.0 0.6 subtract_multiply_fusion.6
  217.5 4.6 fusion.16
  222.1 63.7 %pmax.59 = f32[2048]{0:T(1024)S(1)} all-reduce(f32[2048]{0:T(1024)S(1)} %fusion.16), channel_id=1, replica_groups=mesh['gen'=32,'beam'=8] {'gen'}, use_global_device_ids=true, to_apply=%region_15.0 | all-reduce | flops 2048 | bytes 16384 | tf_op jit(solution)/shard_map/pmax | solution.py:29
  285.8 5.1 exponential_reduce_fusion.4
  290.9 63.7 %psum.73 = f32[2048]{0:T(1024)S(1)} all-reduce(f32[2048]{0:T(1024)S(1)} %exponential_reduce_fusion.4), channel_id=1, replica_groups=mesh['gen'=32,'beam'=8] {'gen'}, use_global_device_ids=true, to_apply=%region_17.0 | all-reduce | flops 2048 | bytes 16384 | tf_op jit(solution)/shard_map/psum | solution.py:30
  354.6 0.6 subtract_multiply_fusion.2
  355.2 4.9 fusion.2
  360.1 16.2 %pmax.60 = f32[1024]{0:T(1024)S(1)} all-reduce(f32[1024]{0:T(1024)S(1)} %fusion.2), channel_id=1, replica_groups=mesh['gen'=32,'beam'=8] {'beam'}, use_global_device_ids=true, to_apply=%region_19.0 | all-reduce | flops 1024 | bytes 8192 | tf_op jit(solution)/shard_map/pmax | solution.py:23
  376.3 5.1 exponential_reduce_fusion.3
  381.4 14.3 %psum.74 = f32[1024]{0:T(1024)S(1)} all-reduce(f32[1024]{0:T(1024)S(1)} %exponential_reduce_fusion.3), channel_id=1, replica_groups=mesh['gen'=32,'beam'=8] {'beam'}, use_global_device_ids=true, to_apply=%region_21.0 | all-reduce | flops 1024 | bytes 8192 | tf_op jit(solution)/shard_map/psum | solution.py:24
  395.8 0.7 subtract_multiply_fusion.5
  396.4 4.7 fusion.17
  401.1 63.7 %pmax.61 = f32[2048]{0:T(1024)S(1)} all-reduce(f32[2048]{0:T(1024)S(1)} %fusion.17), channel_id=1, replica_groups=mesh['gen'=32,'beam'=8] {'gen'}, use_global_device_ids=true, to_apply=%region_23.0 | all-reduce | flops 2048 | bytes 16384 | tf_op jit(solution)/shard_map/pmax | solution.py:29
  464.8 5.2 exponential_reduce_fusion.2
  470.0 63.7 %psum.75 = f32[2048]{0:T(1024)S(1)} all-reduce(f32[2048]{0:T(1024)S(1)} %exponential_reduce_fusion.2), channel_id=1, replica_groups=mesh['gen'=32,'beam'=8] {'gen'}, use_global_device_ids=true, to_apply=%region_25.0 | all-reduce | flops 2048 | bytes 16384 | tf_op jit(solution)/shard_map/psum | solution.py:30
  533.6 0.7 subtract_multiply_fusion.1
  534.3 4.9 fusion.3
  539.2 16.2 %pmax.62 = f32[1024]{0:T(1024)S(1)} all-reduce(f32[1024]{0:T(1024)S(1)} %fusion.3), channel_id=1, replica_groups=mesh['gen'=32,'beam'=8] {'beam'}, use_global_device_ids=true, to_apply=%region_27.0 | all-reduce | flops 1024 | bytes 8192 | tf_op jit(solution)/shard_map/pmax | solution.py:23
  555.4 5.1 exponential_reduce_fusion.1
  560.5 14.2 %psum.76 = f32[1024]{0:T(1024)S(1)} all-reduce(f32[1024]{0:T(1024)S(1)} %exponential_reduce_fusion.1), channel_id=1, replica_groups=mesh['gen'=32,'beam'=8] {'beam'}, use_global_device_ids=true, to_apply=%region_29.0 | all-reduce | flops 1024 | bytes 8192 | tf_op jit(solution)/shard_map/psum | solution.py:24
  574.7 0.7 subtract_multiply_fusion.4
  575.4 4.7 fusion.18
  580.0 63.7 %pmax.63 = f32[2048]{0:T(1024)S(1)} all-reduce(f32[2048]{0:T(1024)S(1)} %fusion.18), channel_id=1, replica_groups=mesh['gen'=32,'beam'=8] {'gen'}, use_global_device_ids=true, to_apply=%region_31.0 | all-reduce | flops 2048 | bytes 16384 | tf_op jit(solution)/shard_map/pmax | solution.py:29
  643.7 5.2 exponential_reduce_fusion
  648.9 63.7 %psum.77 = f32[2048]{0:T(1024)S(1)} all-reduce(f32[2048]{0:T(1024)S(1)} %exponential_reduce_fusion), channel_id=1, replica_groups=mesh['gen'=32,'beam'=8] {'gen'}, use_global_device_ids=true, to_apply=%region_33.0 | all-reduce | flops 2048 | bytes 16384 | tf_op jit(solution)/shard_map/psum | solution.py:30
  712.6 0.7 subtract_multiply_fusion
  713.3 0.0 copy-start.3
  713.3 5.7 fusion.37
  719.0 1.9 copy-done.1
  720.9 2.4 fusion.4
  723.3 0.0 reduce-scatter.5.cloned.1.call-update
  723.3 0.0 reduce-scatter.3.cloned.1.call-start
  723.4 4.5 fusion.11
  727.9 0.0 reduce-scatter.3.cloned.1.call-update
  727.9 0.0 all-reduce.3.cloned.1.call-start
  728.0 92.3 %reduce-scatter.5.cloned.1.call-done = f32[64,128]{1,0:T(8,128)} async-done(((f32[2048,128]{1,0:T(8,128)}), f32[64,128]{1,0:T(8,128)}) %reduce-scatter.5.cloned.1.call-update) | async-done | bytes 32784 | tf_op jit(solution)/shard_map/reduce_scatter | solution.py:85
  820.2 1.0 fusion.25
  821.3 38.7 %reduce-scatter.3.cloned.1.call-done = f32[128,128]{0,1:T(8,128)} async-done(((f32[1024,128]{0,1:T(8,128)}), f32[128,128]{0,1:T(8,128)}) %reduce-scatter.3.cloned.1.call-update) | async-done | bytes 65552 | tf_op jit(solution)/shard_map/reduce_scatter | solution.py:72
  859.9 1.8 convolution_add_fusion
  861.7 0.0 all-reduce.3.cloned.1.call-update
  861.7 0.0 all-reduce.5.cloned.1.call-start
  861.8 71.5 %all-reduce.3.cloned.1.call-done = f32[256,128]{1,0:T(8,128)} async-done(((f32[256,128]{1,0:T(8,128)}), f32[256,128]{1,0:T(8,128)}) %all-reduce.3.cloned.1.call-update) | async-done | bytes 131088 | tf_op jit(solution)/shard_map/psum | solution.py:95
  933.3 0.0 all-reduce.5.cloned.1.call-update
  933.4 111.1 %all-reduce.5.cloned.1.call-done = f32[256,128]{1,0:T(8,128)} async-done(((f32[256,128]{1,0:T(8,128)}), f32[256,128]{1,0:T(8,128)}) %all-reduce.5.cloned.1.call-update) | async-done | bytes 131088 | tf_op jit(solution)/shard_map/psum | solution.py:95
  1044.5 1.6 copy.9
  (5 shorter events, 0.0 us)
Async XLA Ops:
  7.2 1.5 copy-start
  7.2 813.0 %reduce-scatter.5.cloned.1.call-start = ((), (), s32[]{:S(2)}) async-start(), calls=%async_computation.3 | async-start | bytes 1081344 | tf_op jit(solution)/shard_map/reduce_scatter | solution.py:85
  575.4 137.9 %copy-start.2 = (f32[1024]{0:T(1024)}, f32[1024]{0:T(1024)S(1)}, u32[]{:S(2)}) copy-start(f32[1024]{0:T(1024)S(1)} %subtract_multiply_fusion.4) | copy-start | bytes 12292
  713.3 10.0 copy-start.3
  719.0 1.9 copy-start.1
  723.3 136.6 %reduce-scatter.3.cloned.1.call-start = ((), (), s32[]{:S(2)}) async-start(), calls=%async_computation.2 | async-start | bytes 589824 | tf_op jit(solution)/shard_map/reduce_scatter | solution.py:72
  727.9 205.4 %all-reduce.3.cloned.1.call-start = ((), (), s32[]{:S(2)}) async-start(), calls=%async_computation.4 | async-start | bytes 262144 | tf_op jit(solution)/shard_map/psum | solution.py:95
  861.7 182.8 %all-reduce.5.cloned.1.call-start = ((), (), s32[]{:S(2)}) async-start(), calls=%async_computation.5 | async-start | bytes 262144 | tf_op jit(solution)/shard_map/psum | solution.py:95
Sparse Core Ops, SparseCore 0:
  723.5 96.7 reduce-scatter.4
  822.9 36.9 reduce-scatter.2
  862.8 70.4 all-reduce.2
  936.7 107.7 all-reduce.4
